TPU v7x, 128 devices: a whole 4x4x4 slice. The times are simulated.
128 devices in a mesh: pole: 4 (over y_lo, core), dom: 32 (over z, x, y_hi).
Axes of the slice: x: 4, y: 4 (y_hi: 2, y_lo: 2; y = y_hi * 2 + y_lo), z: 4, core: 2. Of those that a mesh axis runs over, the one named last changes fastest.
Arguments:
- initial_block: bfloat16 [32, 8, 512, 256], P('dom'), may hold values from -24 to 24
- coupling: bfloat16 [32, 8, 512, 512], P('dom'), may hold values from -0.125 to 0.125
- pivots: bfloat16 [4, 32, 8, 2, 512, 512], P('pole', 'dom'), may hold values from -0.125 to 0.125
- interface: bfloat16 [4, 32, 3, 2, 512, 512], P('pole', 'dom'), may hold values from -0.1875 to 0.1875
- pole_values: float32 [4, 4], P('pole'), may hold values from 0.5 to 1.5
Outputs:
- filtered_basis: float32 [32, 8, 512, 256], P('dom', 'pole')
- rayleigh: float32 [256, 256], replicated
All inputs are finite; a program needn't handle non-finite values.
Results may differ from a plain program's by a relative error of at most 0.008.
Values sent between devices are 32-bit elements; how exact they have to be, the bound alone decides.
A program may use at most 192 MiB of HBM per device.

v0:
```python
import jax
import jax.numpy as jnp
from jax import lax
from jax.sharding import PartitionSpec as P

B = 512
M = 256


def shifted(x, axis, by):
    length = lax.axis_size(axis)
    pairs = [(i, i + by) for i in range(length) if 0 <= i + by < length]
    return lax.ppermute(x, axis, pairs)


def lower_solve(factor, right_side):
    return lax.linalg.triangular_solve(factor, right_side, left_side=True, lower=True)


def complex_product(matrix, vectors):
    block_order = matrix.shape[1]
    half_width = vectors.shape[1] // 2
    stacked = matrix.reshape(2 * block_order, block_order)
    stacked_out = jnp.dot(stacked, vectors.astype(jnp.bfloat16), preferred_element_type=jnp.float32)
    real_part = stacked_out[:block_order, :half_width] - stacked_out[block_order:, half_width:]
    imag_part = stacked_out[:block_order, half_width:] + stacked_out[block_order:, :half_width]
    return jnp.concatenate([real_part, imag_part], axis=1)


def real_product(matrix, vectors):
    return jnp.dot(matrix, vectors.astype(jnp.bfloat16), preferred_element_type=jnp.float32)


def transposed_product(matrix, vectors):
    return lax.dot_general(
        matrix,
        vectors.astype(jnp.bfloat16),
        (((0,), (0,)), ((), ())),
        preferred_element_type=jnp.float32,
    )


def inner_products(left, right_side):
    return lax.dot_general(
        left,
        right_side,
        (((0,), (0,)), ((), ())),
        precision=lax.Precision.HIGHEST,
        preferred_element_type=jnp.float32,
    )


def partition_solve(inverse, coupled, source):
    previous = jnp.roll(coupled, 1, axis=0)
    initial = jnp.zeros(source.shape[1:], jnp.float32)

    def forward_step(carried, members):
        block_inverse, given, couple_prev = members
        result = complex_product(block_inverse, given + transposed_product(couple_prev, carried))
        return (result, result)

    unused, forward = lax.scan(forward_step, initial, (inverse, source, previous))

    def backward_step(carried, members):
        block_inverse, partial_value, couple_next = members
        result = partial_value + complex_product(block_inverse, real_product(couple_next, carried))
        return (result, result)

    unused, backward = lax.scan(backward_step, initial, (inverse, forward, coupled), reverse=True)
    return backward


def on_device(initial_block, coupling, pivots, interface, pole_values):
    blocks = coupling.shape[1]
    coupled = coupling[0]
    inverse = pivots[0, 0]
    factors = interface[0, 0]
    real_start = initial_block[0].astype(jnp.float32)
    source = jnp.concatenate([real_start, jnp.zeros_like(real_start)], axis=-1)
    first = partition_solve(inverse, coupled, source)
    bottom = first[blocks - 1]
    top = first[0]
    top_next = shifted(top, "dom", -1)
    below = complex_product(factors[0], bottom) - complex_product(factors[1], top_next)
    topmost = lax.axis_index("dom") == lax.axis_size("dom") - 1
    above = jnp.where(
        topmost, jnp.zeros_like(top_next), top_next - complex_product(factors[2], below)
    )
    link = coupled[blocks - 1]
    lifted = transposed_product(link, below)
    arriving = shifted(lifted, "dom", 1)
    update = source.at[0].add(arriving)
    update = update.at[blocks - 1].add(real_product(link, above))
    second = partition_solve(inverse, coupled, update)
    real_z = pole_values[0, 0]
    imag_z = pole_values[0, 1]
    real_w = pole_values[0, 2]
    imag_w = pole_values[0, 3]
    real_x = second[..., :M]
    imag_x = second[..., M:]
    filtered_term = real_w * real_x - imag_w * imag_x
    shifted_term = (
        (real_w * real_z - imag_w * imag_z) * real_x
        - (real_w * imag_z + imag_w * real_z) * imag_x
        - real_w * real_start
    )
    count = blocks // lax.axis_size("pole")
    owned, shifted_owned = (
        lax.psum_scatter(filtered_term[None], "pole", scatter_dimension=1, tiled=True),
        lax.psum_scatter(shifted_term[None], "pole", scatter_dimension=1, tiled=True),
    )
    own_rows = owned[0].reshape(count * B, M)
    gram_part = inner_products(own_rows, own_rows)
    projected_part = inner_products(own_rows, shifted_owned[0].reshape(count * B, M))
    gram_total, projected_total = lax.psum((gram_part, projected_part), ("pole", "dom"))
    row_total = blocks * B * lax.axis_size("dom")
    gram = gram_total / row_total
    projected = projected_total / row_total
    factor = jnp.linalg.cholesky(gram)
    filtered_basis = lower_solve(factor, own_rows.T).T.reshape(1, count, B, M)
    middle = lower_solve(factor, projected)
    rayleigh = lower_solve(factor, middle.T).T
    return (filtered_basis, rayleigh)


def solution(mesh):
    in_specs = (
        P("dom", None, None, None),
        P("dom", None, None, None),
        P("pole", "dom", None, None, None, None),
        P("pole", "dom", None, None, None, None),
        P("pole", None),
    )
    out_specs = (P("dom", "pole", None, None), P())
    return jax.shard_map(
        on_device, mesh=mesh, in_specs=in_specs, out_specs=out_specs, check_vma=False
    )
```

profile of v0, /device:TPU:1, one launch (start us, length us, event | category | flops | bytes accessed | tf_op | source)
XLA Modules:
  0.0 714.1 jit_solution(7158494593496729926)
XLA Ops:
  7.2 4.2 slice_bitcast_fusion
  12.5 2.9 copy.17
  18.0 4.2 concatenate.76
  24.6 4.3 broadcast.158.clone.2
  29.7 65.3 %while.65 = (s32[]{:T(128)}, bf16[512,512]{0,1:T(8,128)(2,1)}, f32[8,512,512]{1,2,0:T(8,128)}, bf16[8,2,512,512]{3,2,1,0:T(8,128)(2,1)}, f32[8,512,512]{1,2,0:T(8,128)}, /*index=5*/bf16[8,512,512]{2,1,0:T(8,128)(2,1)}, s32[]{:T(128)}) while((s32[]{:T(128)}, bf16[512,512]{0,1:T(8,128)(2,1)}, f32[8,512,512]{1,2,0:T(8,128)}, ...), condition=%wide.region_1.2_spmd, body=%wide.region_0.1_spmd.sunk | while | flops 806617088 | bytes 17302612 | solution.py:62
  33.6 2.7 fusion.131
  41.8 2.7 fusion.131
  50.0 2.7 fusion.131
  58.1 2.7 fusion.131
  66.3 2.7 fusion.131
  74.5 2.7 fusion.131
  82.6 2.7 fusion.131
  90.8 2.7 fusion.131
  95.0 4.3 broadcast.158.clone.1
  99.3 67.7 %while.68 = (s32[]{:T(128)}, bf16[512,512]{0,1:T(8,128)(2,1)}, f32[8,512,512]{1,2,0:T(8,128)}, f32[8,512,512]{1,2,0:T(8,128)}, bf16[8,2,512,512]{3,2,1,0:T(8,128...) while((s32[]{:T(128)}, bf16[512,512]{0,1:T(8,128)(2,1)}, ...), condition=%wide.region_3.4_spmd.clone, body=%wide.region_2.3_spmd.clone.sunk | while | flops 807403520 | bytes 15204483 | solution.py:69
  103.0 2.5 fusion.140
  120.0 2.4 fusion.140
  136.9 2.4 fusion.140
  173.9 22.7 %collective-permute-done = f32[512,512]{0,1:T(8,128)S(1)} collective-permute-done((f32[512,512]{0,1:T(8,128)S(1)}, f32[512,512]{0,1:T(8,128)S(1)}, u32[]{:S(2)}, u32[]{:S(2)}) %collective-permute-start) | collective-permute-done | bytes 1048608 | tf_op jit(solution)/shard_map/ppermute | solution.py:13
  197.8 2.5 convolution_bitcast_fusion.4
  200.3 7.2 %collective-permute-start.1 = (f32[512,512]{0,1:T(8,128)}, f32[512,512]{0,1:T(8,128)}, u32[]{:S(2)}, u32[]{:S(2)}) collective-permute-start(f32[512,512]{0,1:T(8,128)} %convolution_bitcast_fusion.4), channel_id=1, source_target_pairs={{0,1},{1,2},{2,3},{3,4},{4,5},{5,6},{6,7},{7,8},{8,9},{9,10},{10,1... | collective-permute-start | bytes 3145736 | tf_op jit(solution)/shard_map/ppermute | solution.py:13
  213.9 13.3 %collective-permute-done.1 = f32[512,512]{0,1:T(8,128)} collective-permute-done((f32[512,512]{0,1:T(8,128)}, f32[512,512]{0,1:T(8,128)}, u32[]{:S(2)}, u32[]{:S(2)}) %collective-permute-start.1) | collective-permute-done | bytes 1048608 | tf_op jit(solution)/shard_map/ppermute | solution.py:13
  229.5 2.9 fusion.52
  232.4 4.3 broadcast.158.clone
  237.6 65.4 %while.66 = (s32[]{:T(128)}, bf16[512,512]{0,1:T(8,128)(2,1)}, f32[8,512,512]{1,2,0:T(8,128)}, bf16[8,2,512,512]{3,2,1,0:T(8,128)(2,1)}, f32[8,512,512]{1,2,0:T(8,128)}, /*index=5*/bf16[8,512,512]{2,1,0:T(8,128)(2,1)}, s32[]{:T(128)}) while((s32[]{:T(128)}, bf16[512,512]{0,1:T(8,128)(2,1)}, f32[8,512,512]{1,2,0:T(8,128)}, ...), condition=%wide.region_5.6_spmd, body=%wide.region_4.5_spmd.sunk | while | flops 806617088 | bytes 17302612 | solution.py:62
  241.5 2.7 fusion.135
  249.7 2.7 fusion.135
  257.8 2.7 fusion.135
  266.0 2.7 fusion.135
  274.2 2.7 fusion.135
  282.5 2.7 fusion.135
  290.6 2.7 fusion.135
  298.8 2.7 fusion.135
  303.0 4.3 broadcast.158
  307.4 67.7 %while.69 = (s32[]{:T(128)}, bf16[512,512]{0,1:T(8,128)(2,1)}, f32[8,512,512]{1,2,0:T(8,128)}, f32[8,512,512]{1,2,0:T(8,128)}, bf16[8,2,512,512]{3,2,1,0:T(8,128...) while((s32[]{:T(128)}, bf16[512,512]{0,1:T(8,128)(2,1)}, ...), condition=%wide.region_7.8_spmd.clone, body=%wide.region_6.7_spmd.clone.sunk | while | flops 807403520 | bytes 15204483 | solution.py:69
  311.1 2.5 fusion.144
  328.0 2.4 fusion.144
  375.0 9.9 %subtract_bitcast_fusion = (f32[1,8,512,256]{2,3,1,0:T(8,128)}, f32[1,8,512,256]{2,3,1,0:T(8,128)}) fusion(f32[8,512,512]{1,2,0:T(8,128)} %get-tuple-element.338, f32[]{:T(128)S(6)} %add.169, f32[]{:T(128)S(6)} %sub.71, f32[]{:T(128)} %bitcast.8, bf16[1,8,512,256]{2,3,1,0:T(8,128)(2,1)} %copy-done.2, f32[]{:T(128)} %bitcast.27), kind=kLoop, calls=%fused_computation.61 | loop fusion | flops 9437184 | bytes 18874384 | tf_op jit(solution)/shard_map/broadcast_in_dim | solution.py:110
  386.0 51.5 %reduce-scatter.3.cloned.1.call-done = f32[1,2,512,256]{2,3,1,0:T(8,128)} async-done(((f32[1,8,512,256]{2,3,1,0:T(8,128)}), f32[1,2,512,256]{2,3,1,0:T(8,128)}) %reduce-scatter.3.cloned.1.call-update) | async-done | bytes 1048592 | tf_op jit(solution)/shard_map/reduce_scatter | solution.py:109
  437.4 3.4 convolution_bitcast_fusion.6
  440.8 45.5 %reduce-scatter.5.cloned.1.call-done = f32[1,2,512,256]{2,3,1,0:T(8,128)} async-done(((f32[1,8,512,256]{2,3,1,0:T(8,128)}), f32[1,2,512,256]{2,3,1,0:T(8,128)}) %reduce-scatter.5.cloned.1.call-update) | async-done | bytes 1048592 | tf_op jit(solution)/shard_map/reduce_scatter | solution.py:110
  486.3 3.3 convolution_bitcast_fusion.5
  490.0 148.1 %all-reduce.5.cloned.1.call-done = (f32[256,256]{0,1:T(8,128)}, f32[256,256]{0,1:T(8,128)}) async-done(((f32[256,256]{0,1:T(8,128)}, f32[256,256]{0,1:T(8,128)}), (f32[256,256]{0,1:T(8,128)}, f32[256,256]{0,1:T(8,128)})) %all-reduce.5.cloned.1.call-update) | async-done | bytes 524304 | tf_op jit(solution)/shard_map/psum | solution.py:115
  640.3 11.7 %cholesky.50 = f32[128,128]{1,0:T(8,128)S(1)} custom-call(f32[128,128]{1,0:T(8,128)S(1)} %cholesky.118), custom_call_target="Cholesky" | custom-call | tf_op jit(solution)/shard_map/jit(cholesky)/cholesky | solution.py:119
  652.1 9.8 %custom-call.17 = f32[1,128,128]{1,2,0:T(8,128)S(1)} custom-call(f32[1,128,128]{2,1,0:T(8,128)S(1)} %get-tuple-element.519), custom_call_target="InvertDiagBlocksLowerTriangular" | custom-call | tf_op jit(solution)/shard_map/jit(cholesky)/cholesky | solution.py:119
  662.4 11.9 %cholesky.105 = f32[128,128]{1,0:T(8,128)S(1)} custom-call(f32[128,128]{1,0:T(8,128)S(1)} %convolution_subtract_fusion.3), custom_call_target="Cholesky" | custom-call | tf_op jit(solution)/shard_map/jit(cholesky)/cholesky | solution.py:119
  677.0 4.0 while.67
  681.0 19.7 %custom-call.18 = f32[2,128,128]{1,2,0:T(8,128)S(1)} custom-call(f32[2,128,128]{2,1,0:T(8,128)S(1)} %get-tuple-element.354), custom_call_target="InvertDiagBlocksLowerTriangular" | custom-call | tf_op jit(solution)/shard_map/triangular_solve | solution.py:17
  (228 shorter events, 246.0 us)
Async XLA Ops:
  7.2 430.3 %reduce-scatter.3.cloned.1.call-start = ((), (), s32[]{:S(2)}) async-start(), calls=%async_computation.2 | async-start | bytes 5242880 | tf_op jit(solution)/shard_map/reduce_scatter | solution.py:109
  15.4 6.9 copy-start.2
  15.9 2.1 copy-start
  18.0 4.2 copy-start.3
  168.3 28.2 %collective-permute-start = (f32[512,512]{0,1:T(8,128)S(1)}, f32[512,512]{0,1:T(8,128)S(1)}, u32[]{:S(2)}, u32[]{:S(2)}) collective-permute-start(f32[512,512]{0,1:T(8,128)S(1)} %slice_bitcast_fusion.1), channel_id=1, source_target_pairs={{1,0},{2,1},{3,2},{4,3},{5,4},{6,5},{7,6},{8,7},{9,8},{10,9},{11,1... | collective-permute-start | bytes 3145736 | tf_op jit(solution)/shard_map/ppermute | solution.py:13
  197.3 10.2 %copy-start.5 = (f32[1,4]{1,0:T(1,128)S(1)}, f32[1,4]{1,0:T(1,128)}, u32[]{:S(2)}) copy-start(f32[1,4]{1,0:T(1,128)} %param.23) | copy-start | bytes 52
  200.3 26.9 %collective-permute-start.1 = (f32[512,512]{0,1:T(8,128)}, f32[512,512]{0,1:T(8,128)}, u32[]{:S(2)}, u32[]{:S(2)}) collective-permute-start(f32[512,512]{0,1:T(8,128)} %convolution_bitcast_fusion.4), channel_id=1, source_target_pairs={{0,1},{1,2},{2,3},{3,4},{4,5},{5,6},{6,7},{7,8},{8,9},{9,10},{10,1... | collective-permute-start | bytes 3145736 | tf_op jit(solution)/shard_map/ppermute | solution.py:13
  212.9 14.2 %copy-start.1 = (f32[8,512,256]{1,2,0:T(8,128)S(1)}, f32[8,512,256]{1,2,0:T(8,128)}, u32[]{:S(2)}) copy-start(f32[8,512,256]{1,2,0:T(8,128)} %copy-done) | copy-start | bytes 12582916
  385.0 101.3 %reduce-scatter.5.cloned.1.call-start = ((), (), s32[]{:S(2)}) async-start(), calls=%async_computation.3 | async-start | bytes 5242880 | tf_op jit(solution)/shard_map/reduce_scatter | solution.py:110
  385.8 252.4 %all-reduce.5.cloned.1.call-start = ((), (), s32[]{:S(2)}) async-start(), calls=%async_computation.4 | async-start | bytes 1048576 | tf_op jit(solution)/shard_map/psum | solution.py:115
  437.4 52.2 %copy-start.4 = (f32[1,2,512,256]{2,3,1,0:T(8,128)S(1)}, f32[1,2,512,256]{2,3,1,0:T(8,128)}, u32[]{:S(2)}) copy-start(f32[1,2,512,256]{2,3,1,0:T(8,128)} %reduce-scatter.3.cloned.1.call-done) | copy-start | bytes 3145732
Sparse Core Ops, SparseCore 0:
  385.1 52.2 reduce-scatter.2
  440.0 46.3 reduce-scatter.4
  491.8 146.2 all-reduce.4
where the time goes:
time: 726 us; the launch traced here: 714 us
  waiting for transfers between devices  282 us (39%)
  other arithmetic  176 us (24%)
  local copies, waits for them, and re-layouts  127 us (17%)
  matrix products  99.8 us (14%)
  between operations  20.4 us (3%)
  starting transfers between devices  8.82 us (1%)
    psum x1, waiting for transfers between devices, on_device(): lax.psum((gram_part, projected_part), ('pole', 'dom'))  148 us
    dot_general x35, matrix products, complex_product(): jnp.dot(stacked, vectors.astype(jnp.bfloat16), preferred_element_type=jnp...  83.1 us
    dynamic_slice x64, local copies, waits for them, and re-layouts, partition_solve(): lax.scan(forward_step, initial, (inverse, source, previous))  82.9 us
    dynamic_update_slice x32, other arithmetic, partition_solve(): lax.scan(forward_step, initial, (inverse, source, previous))  60.9 us
    reduce_scatter x1, waiting for transfers between devices, on_device(): lax.psum_scatter(filtered_term[None], 'pole', scatter_dimension=1, tiled=...  51.5 us
    reduce_scatter x1, waiting for transfers between devices, on_device(): lax.psum_scatter(shifted_term[None], 'pole', scatter_dimension=1, tiled=T...  45.5 us
    ppermute x2, waiting for transfers between devices, shifted(): return lax.ppermute(x, axis, pairs)  36 us
    add x16, other arithmetic, backward_step(): partial_value + complex_product(block_inverse, real_product(couple_next,...  35.2 us
  transfers between devices with their start and end apart: 5, of which 5 were waited for; matrix products, arithmetic and copies ran while one was open for 1% of the time, Pallas kernels for 0%

commit v1 on v0

--- a/solution.py
+++ b/solution.py
@@ -2,9 +2,14 @@
 import jax.numpy as jnp
 from jax import lax
 from jax.sharding import PartitionSpec as P
+from jax.lax import psum
 
 B = 512
 M = 256
+
+
+def point_slots(body, link_axis, row_axis):
+    return psum(psum(body, axis_name=link_axis), row_axis)
 
 
 def shifted(x, axis, by):
@@ -112,7 +117,7 @@
     own_rows = owned[0].reshape(count * B, M)
     gram_part = inner_products(own_rows, own_rows)
     projected_part = inner_products(own_rows, shifted_owned[0].reshape(count * B, M))
-    gram_total, projected_total = lax.psum((gram_part, projected_part), ("pole", "dom"))
+    gram_total, projected_total = point_slots((gram_part, projected_part), "dom", "pole")
     row_total = blocks * B * lax.axis_size("dom")
     gram = gram_total / row_total
     projected = projected_total / row_total

time: 726 us -> 970 us (1.34)
  waiting for transfers between devices: 282 us -> 525 us
    psum x1 -> x2, waiting for transfers between devices: 148 us -> 392 us  [point_slots(): return psum(psum(body, axis_name=link_axis), row_axis)]
  transfers between devices with their start and end apart: 5 -> 6, of which waited for: 5 -> 6; matrix products, arithmetic and copies ran while one was open for 1% -> 1% of each run, Pallas kernels for 0% -> 0%
where the time goes in v1:
time: 970 us; the launch traced here: 958 us
  waiting for transfers between devices  525 us (54%)
  other arithmetic  176 us (18%)
  local copies, waits for them, and re-layouts  127 us (13%)
  matrix products  99.8 us (10%)
  between operations  20.6 us (2%)
    psum x2, waiting for transfers between devices, point_slots(): return psum(psum(body, axis_name=link_axis), row_axis)  392 us
    dot_general x35, matrix products, complex_product(): jnp.dot(stacked, vectors.astype(jnp.bfloat16), preferred_element_type=jnp...  83 us
    dynamic_slice x64, local copies, waits for them, and re-layouts, partition_solve(): lax.scan(forward_step, initial, (inverse, source, previous))  82.9 us
    dynamic_update_slice x32, other arithmetic, partition_solve(): lax.scan(forward_step, initial, (inverse, source, previous))  60.9 us
    reduce_scatter x1, waiting for transfers between devices, on_device(): lax.psum_scatter(filtered_term[None], 'pole', scatter_dimension=1, tiled=...  51.7 us
    reduce_scatter x1, waiting for transfers between devices, on_device(): lax.psum_scatter(shifted_term[None], 'pole', scatter_dimension=1, tiled=T...  45.5 us
    ppermute x2, waiting for transfers between devices, shifted(): return lax.ppermute(x, axis, pairs)  35.8 us
    add x16, other arithmetic, backward_step(): partial_value + complex_product(block_inverse, real_product(couple_next,...  35.4 us
  transfers between devices with their start and end apart: 6, of which 6 were waited for; matrix products, arithmetic and copies ran while one was open for 1% of the time, Pallas kernels for 0%

profile of v1, /device:TPU:1, one launch (start us, length us, event | category | flops | bytes accessed | tf_op | source)
XLA Modules:
  0.0 958.2 jit_solution(1234657980538290111)
XLA Ops:
  7.2 4.2 slice_bitcast_fusion
  12.5 2.9 copy.17
  18.0 4.2 concatenate.76
  24.6 4.3 broadcast.158.clone.2
  29.8 65.2 %while.65 = (s32[]{:T(128)}, bf16[512,512]{0,1:T(8,128)(2,1)}, f32[8,512,512]{1,2,0:T(8,128)}, bf16[8,2,512,512]{3,2,1,0:T(8,128)(2,1)}, f32[8,512,512]{1,2,0:T(8,128)}, /*index=5*/bf16[8,512,512]{2,1,0:T(8,128)(2,1)}, s32[]{:T(128)}) while((s32[]{:T(128)}, bf16[512,512]{0,1:T(8,128)(2,1)}, f32[8,512,512]{1,2,0:T(8,128)}, ...), condition=%wide.region_1.2_spmd, body=%wide.region_0.1_spmd.sunk | while | flops 806617088 | bytes 17302612 | solution.py:67
  33.7 2.7 fusion.131
  41.8 2.7 fusion.131
  49.9 2.7 fusion.131
  58.1 2.7 fusion.131
  66.3 2.7 fusion.131
  74.5 2.7 fusion.131
  82.6 2.7 fusion.131
  90.8 2.7 fusion.131
  95.0 4.3 broadcast.158.clone.1
  99.3 67.8 %while.68 = (s32[]{:T(128)}, bf16[512,512]{0,1:T(8,128)(2,1)}, f32[8,512,512]{1,2,0:T(8,128)}, f32[8,512,512]{1,2,0:T(8,128)}, bf16[8,2,512,512]{3,2,1,0:T(8,128...) while((s32[]{:T(128)}, bf16[512,512]{0,1:T(8,128)(2,1)}, ...), condition=%wide.region_3.4_spmd.clone, body=%wide.region_2.3_spmd.clone.sunk | while | flops 807403520 | bytes 15204483 | solution.py:74
  103.0 2.5 fusion.140
  120.0 2.4 fusion.140
  174.0 22.7 %collective-permute-done = f32[512,512]{0,1:T(8,128)S(1)} collective-permute-done((f32[512,512]{0,1:T(8,128)S(1)}, f32[512,512]{0,1:T(8,128)S(1)}, u32[]{:S(2)}, u32[]{:S(2)}) %collective-permute-start) | collective-permute-done | bytes 1048608 | tf_op jit(solution)/shard_map/ppermute | solution.py:18
  197.9 2.5 convolution_bitcast_fusion.4
  200.4 7.2 collective-permute-start.1
  214.1 13.1 %collective-permute-done.1 = f32[512,512]{0,1:T(8,128)} collective-permute-done((f32[512,512]{0,1:T(8,128)}, f32[512,512]{0,1:T(8,128)}, u32[]{:S(2)}, u32[]{:S(2)}) %collective-permute-start.1) | collective-permute-done | bytes 1048608 | tf_op jit(solution)/shard_map/ppermute | solution.py:18
  229.6 2.9 fusion.52
  232.5 4.3 broadcast.158.clone
  237.7 65.5 %while.66 = (s32[]{:T(128)}, bf16[512,512]{0,1:T(8,128)(2,1)}, f32[8,512,512]{1,2,0:T(8,128)}, bf16[8,2,512,512]{3,2,1,0:T(8,128)(2,1)}, f32[8,512,512]{1,2,0:T(8,128)}, /*index=5*/bf16[8,512,512]{2,1,0:T(8,128)(2,1)}, s32[]{:T(128)}) while((s32[]{:T(128)}, bf16[512,512]{0,1:T(8,128)(2,1)}, f32[8,512,512]{1,2,0:T(8,128)}, ...), condition=%wide.region_5.6_spmd, body=%wide.region_4.5_spmd.sunk | while | flops 806617088 | bytes 17302612 | solution.py:67
  241.6 2.7 fusion.135
  249.7 2.7 fusion.135
  257.9 2.7 fusion.135
  266.1 2.7 fusion.135
  274.3 2.7 fusion.135
  282.6 2.7 fusion.135
  290.7 2.7 fusion.135
  298.9 2.7 fusion.135
  303.2 4.3 broadcast.158
  307.5 67.7 %while.69 = (s32[]{:T(128)}, bf16[512,512]{0,1:T(8,128)(2,1)}, f32[8,512,512]{1,2,0:T(8,128)}, f32[8,512,512]{1,2,0:T(8,128)}, bf16[8,2,512,512]{3,2,1,0:T(8,128...) while((s32[]{:T(128)}, bf16[512,512]{0,1:T(8,128)(2,1)}, ...), condition=%wide.region_7.8_spmd.clone, body=%wide.region_6.7_spmd.clone.sunk | while | flops 807403520 | bytes 15204483 | solution.py:74
  311.2 2.5 fusion.144
  370.6 2.4 fusion.144
  375.3 10.0 %subtract_bitcast_fusion = (f32[1,8,512,256]{2,3,1,0:T(8,128)}, f32[1,8,512,256]{2,3,1,0:T(8,128)}) fusion(f32[8,512,512]{1,2,0:T(8,128)} %get-tuple-element.338, f32[]{:T(128)S(6)} %add.173, f32[]{:T(128)S(6)} %sub.71, f32[]{:T(128)} %bitcast.8, bf16[1,8,512,256]{2,3,1,0:T(8,128)(2,1)} %copy-done.2, f32[]{:T(128)} %bitcast.27), kind=kLoop, calls=%fused_computation.61 | loop fusion | flops 9437184 | bytes 18874384 | tf_op jit(solution)/shard_map/broadcast_in_dim | solution.py:115
  386.1 51.7 %reduce-scatter.3.cloned.1.call-done = f32[1,2,512,256]{2,3,1,0:T(8,128)} async-done(((f32[1,8,512,256]{2,3,1,0:T(8,128)}), f32[1,2,512,256]{2,3,1,0:T(8,128)}) %reduce-scatter.3.cloned.1.call-update) | async-done | bytes 1048592 | tf_op jit(solution)/shard_map/reduce_scatter | solution.py:114
  437.7 3.4 convolution_bitcast_fusion.6
  441.1 45.5 %reduce-scatter.5.cloned.1.call-done = f32[1,2,512,256]{2,3,1,0:T(8,128)} async-done(((f32[1,8,512,256]{2,3,1,0:T(8,128)}), f32[1,2,512,256]{2,3,1,0:T(8,128)}) %reduce-scatter.5.cloned.1.call-update) | async-done | bytes 1048592 | tf_op jit(solution)/shard_map/reduce_scatter | solution.py:115
  486.6 3.3 convolution_bitcast_fusion.5
  490.1 329.1 %all-reduce.7.cloned.1.call-done = (f32[256,256]{0,1:T(8,128)}, f32[256,256]{0,1:T(8,128)}) async-done(((f32[256,256]{0,1:T(8,128)}, f32[256,256]{0,1:T(8,128)}), (f32[256,256]{0,1:T(8,128)}, f32[256,256]{0,1:T(8,128)})) %all-reduce.7.cloned.1.call-update) | async-done | bytes 524304 | tf_op jit(solution)/shard_map/psum | solution.py:12
  819.6 62.5 %all-reduce.9.cloned.1.call-done = (f32[256,256]{0,1:T(8,128)}, f32[256,256]{0,1:T(8,128)}) async-done(((f32[256,256]{0,1:T(8,128)}, f32[256,256]{0,1:T(8,128)}), (f32[256,256]{0,1:T(8,128)}, f32[256,256]{0,1:T(8,128)})) %all-reduce.9.cloned.1.call-update) | async-done | bytes 524304 | tf_op jit(solution)/shard_map/psum | solution.py:12
  884.3 11.7 %cholesky.50 = f32[128,128]{1,0:T(8,128)S(1)} custom-call(f32[128,128]{1,0:T(8,128)S(1)} %cholesky.118), custom_call_target="Cholesky" | custom-call | tf_op jit(solution)/shard_map/jit(cholesky)/cholesky | solution.py:124
  896.1 9.8 %custom-call.17 = f32[1,128,128]{1,2,0:T(8,128)S(1)} custom-call(f32[1,128,128]{2,1,0:T(8,128)S(1)} %get-tuple-element.521), custom_call_target="InvertDiagBlocksLowerTriangular" | custom-call | tf_op jit(solution)/shard_map/jit(cholesky)/cholesky | solution.py:124
  906.4 11.7 %cholesky.105 = f32[128,128]{1,0:T(8,128)S(1)} custom-call(f32[128,128]{1,0:T(8,128)S(1)} %convolution_subtract_fusion.3), custom_call_target="Cholesky" | custom-call | tf_op jit(solution)/shard_map/jit(cholesky)/cholesky | solution.py:124
  920.8 4.2 while.67
  925.0 19.7 %custom-call.18 = f32[2,128,128]{1,2,0:T(8,128)S(1)} custom-call(f32[2,128,128]{2,1,0:T(8,128)S(1)} %get-tuple-element.354), custom_call_target="InvertDiagBlocksLowerTriangular" | custom-call | tf_op jit(solution)/shard_map/triangular_solve | solution.py:22
  (231 shorter events, 248.8 us)
Async XLA Ops:
  7.2 430.6 %reduce-scatter.3.cloned.1.call-start = ((), (), s32[]{:S(2)}) async-start(), calls=%async_computation.2 | async-start | bytes 5242880 | tf_op jit(solution)/shard_map/reduce_scatter | solution.py:114
  15.4 6.9 copy-start.2
  16.0 2.1 copy-start
  18.0 4.3 copy-start.3
  168.4 28.2 %collective-permute-start = (f32[512,512]{0,1:T(8,128)S(1)}, f32[512,512]{0,1:T(8,128)S(1)}, u32[]{:S(2)}, u32[]{:S(2)}) collective-permute-start(f32[512,512]{0,1:T(8,128)S(1)} %slice_bitcast_fusion.1), channel_id=1, source_target_pairs={{1,0},{2,1},{3,2},{4,3},{5,4},{6,5},{7,6},{8,7},{9,8},{10,9},{11,1... | collective-permute-start | bytes 3145736 | tf_op jit(solution)/shard_map/ppermute | solution.py:18
  197.4 10.2 %copy-start.5 = (f32[1,4]{1,0:T(1,128)S(1)}, f32[1,4]{1,0:T(1,128)}, u32[]{:S(2)}) copy-start(f32[1,4]{1,0:T(1,128)} %param.23) | copy-start | bytes 52
  200.4 26.9 %collective-permute-start.1 = (f32[512,512]{0,1:T(8,128)}, f32[512,512]{0,1:T(8,128)}, u32[]{:S(2)}, u32[]{:S(2)}) collective-permute-start(f32[512,512]{0,1:T(8,128)} %convolution_bitcast_fusion.4), channel_id=1, source_target_pairs={{0,1},{1,2},{2,3},{3,4},{4,5},{5,6},{6,7},{7,8},{8,9},{9,10},{10,1... | collective-permute-start | bytes 3145736 | tf_op jit(solution)/shard_map/ppermute | solution.py:18
  213.2 14.1 %copy-start.1 = (f32[8,512,256]{1,2,0:T(8,128)S(1)}, f32[8,512,256]{1,2,0:T(8,128)}, u32[]{:S(2)}) copy-start(f32[8,512,256]{1,2,0:T(8,128)} %copy-done) | copy-start | bytes 12582916
  385.3 101.4 %reduce-scatter.5.cloned.1.call-start = ((), (), s32[]{:S(2)}) async-start(), calls=%async_computation.3 | async-start | bytes 5242880 | tf_op jit(solution)/shard_map/reduce_scatter | solution.py:115
  386.0 433.2 %all-reduce.7.cloned.1.call-start = ((), (), s32[]{:S(2)}) async-start(), calls=%async_computation.4 | async-start | bytes 1048576 | tf_op jit(solution)/shard_map/psum | solution.py:12
  437.7 381.5 %copy-start.4 = (f32[1,2,512,256]{2,3,1,0:T(8,128)S(1)}, f32[1,2,512,256]{2,3,1,0:T(8,128)}, u32[]{:S(2)}) copy-start(f32[1,2,512,256]{2,3,1,0:T(8,128)} %reduce-scatter.3.cloned.1.call-done) | copy-start | bytes 3145732
  489.9 392.2 %all-reduce.9.cloned.1.call-start = ((), (), s32[]{:S(2)}) async-start(), calls=%async_computation.5 | async-start | bytes 1048576 | tf_op jit(solution)/shard_map/psum | solution.py:12
Sparse Core Ops, SparseCore 0:
  385.4 52.3 reduce-scatter.2
  440.3 46.3 reduce-scatter.4
  490.0 329.1 all-reduce.6
  821.8 60.3 all-reduce.8
